TPU v7x, 32 devices: a whole 2x2x4 slice. The times are simulated.
32 devices in a mesh: dp: 32 (over z, y, x, core).
Axes of the slice: x: 2, y: 2, z: 4, core: 2. Of those that a mesh axis runs over, the one named last changes fastest.
Arguments:
- tokens: bfloat16 [32, 1024, 512], P('dp'), may hold values from -6 to 6
- memory: bfloat16 [32, 1024, 512], P('dp'), may hold values from -6 to 6
- cotangent: bfloat16 [32, 1024, 512], P('dp'), may hold values from -6 to 6
- dec_segments: int32 [32, 1024], P('dp'), may hold values from -1 to 15, as said below
- mem_segments: int32 [32, 1024], P('dp'), may hold values from -1 to 15, as said below
- time_steps: int32 [32, 16], P('dp'), may hold values from 0 to 49
- time_table: bfloat16 [512, 50], P('dp'), may hold values from -3 to 3
- first_gain: bfloat16 [512], P('dp'), may hold values from 0.25 to 1.75
- first_bias: bfloat16 [512], P('dp'), may hold values from -2 to 2
- self_query: bfloat16 [512, 512], P('dp'), may hold values from -0.25 to 0.25
- self_key: bfloat16 [512, 512], P('dp'), may hold values from -0.25 to 0.25
- self_value: bfloat16 [512, 512], P('dp'), may hold values from -0.25 to 0.25
- self_out: bfloat16 [512, 512], P('dp'), may hold values from -1.5 to 1.5
- cross_query: bfloat16 [512, 512], P('dp'), may hold values from -0.25 to 0.25
- cross_key: bfloat16 [512, 512], P('dp'), may hold values from -0.25 to 0.25
- cross_value: bfloat16 [512, 512], P('dp'), may hold values from -0.25 to 0.25
- cross_out: bfloat16 [512, 512], P('dp'), may hold values from -1.5 to 1.5
- second_gain: bfloat16 [512], P('dp'), may hold values from 0.25 to 1.75
- second_bias: bfloat16 [512], P('dp'), may hold values from -2 to 2
- expand_weight: bfloat16 [512, 2048], P('dp'), may hold values from -0.25 to 0.25
- expand_bias: bfloat16 [2048], P('dp'), may hold values from -3 to 3
- shrink_weight: bfloat16 [2048, 512], P('dp'), may hold values from -0.25 to 0.25
- shrink_bias: bfloat16 [512], P('dp'), may hold values from -2 to 2
Outputs:
- layer_out: bfloat16 [32, 1024, 512], P('dp')
- tokens_grad: float32 [32, 1024, 512], P('dp')
- memory_grad: float32 [32, 1024, 512], P('dp')
- time_table_grad: float32 [512, 50], P('dp')
- first_gain_grad: float32 [512], P('dp')
- first_bias_grad: float32 [512], P('dp')
- self_query_grad: float32 [512, 512], P('dp')
- self_key_grad: float32 [512, 512], P('dp')
- self_value_grad: float32 [512, 512], P('dp')
- self_out_grad: float32 [512, 512], P('dp')
- cross_query_grad: float32 [512, 512], P('dp')
- cross_key_grad: float32 [512, 512], P('dp')
- cross_value_grad: float32 [512, 512], P('dp')
- cross_out_grad: float32 [512, 512], P('dp')
- second_gain_grad: float32 [512], P('dp')
- second_bias_grad: float32 [512], P('dp')
- expand_weight_grad: float32 [512, 2048], P('dp')
- expand_bias_grad: float32 [2048], P('dp')
- shrink_weight_grad: float32 [2048, 512], P('dp')
- shrink_bias_grad: float32 [512], P('dp')
Inputs may be any that keep to these rules, and one draw needn't show every extreme that they name: `dec_segments`: in each row the ids are 0 to 15, never falling, each present, over a prefix of the row; the remaining slots (at least one) hold -1. `mem_segments`: in each row the ids are 0 to 15, never falling, each present, over a prefix of the row; the remaining slots (at least one) hold -1.
All inputs are finite; a program needn't handle non-finite values.
Results may differ from a plain program's by a relative error of at most 0.03.
The roundings to bfloat16 on the way count: a program that leaves them out, or rounds other values in their place, can miss the bound.
Values may be sent and summed in bfloat16 or wider, within the bound.
A program may use at most 192 MiB of HBM per device.

v0:
```python
import jax
import jax.numpy as jnp
from jax import lax
from jax.sharding import PartitionSpec as P

HEADS = 8


EPS = 1e-05
NEG = -1e30
HIGH = lax.Precision.HIGHEST
FLOAT_TYPE = jnp.float32
HALF_TYPE = jnp.bfloat16


def layer_norm(values, gain, offset):
    centre_mean = jnp.mean(values, axis=-1, keepdims=True)
    centred = values - centre_mean
    spread_var = jnp.mean(centred * centred, axis=-1, keepdims=True)
    return centred * lax.rsqrt(spread_var + EPS) * gain + offset


def exact_gelu(values):
    return jax.nn.gelu(values, approximate=False)


def product(left, right):
    return jnp.dot(left, right, preferred_element_type=FLOAT_TYPE)


def product_left_t(left, right):
    return lax.dot_general(left, right, (((0,), (0,)), ((), ())), preferred_element_type=FLOAT_TYPE)


def product_right_t(left, right):
    return lax.dot_general(left, right, (((1,), (1,)), ((), ())), preferred_element_type=FLOAT_TYPE)


def slot_onehot(segments, steps_given, step_count):
    seg_count = steps_given.shape[1]
    seg_picks = (
        segments[:, :, None] == jnp.arange(seg_count, dtype=jnp.int32)[None, None, :]
    ).astype(FLOAT_TYPE)
    step_picks = (
        steps_given[:, :, None] == jnp.arange(step_count, dtype=jnp.int32)[None, None, :]
    ).astype(FLOAT_TYPE)
    return jnp.einsum("rls,rst->rlt", seg_picks, step_picks, precision=HIGH).reshape(-1, step_count)


def attend_forward(paired):
    query_rows, key_rows, value_rows, seg_query, seg_keys = paired
    length, model_width = query_rows.shape
    head_size = model_width // HEADS
    block_rows = min(512, length)
    q_blocks = query_rows.reshape(length // block_rows, block_rows, HEADS, head_size)
    s_blocks = seg_query.reshape(length // block_rows, block_rows)
    key_heads = key_rows.reshape(-1, HEADS, head_size)
    value_heads = value_rows.reshape(-1, HEADS, head_size)

    def one_block(block_items):
        q_part, s_part = block_items
        scores = jnp.einsum("qhd,khd->hqk", q_part, key_heads, preferred_element_type=FLOAT_TYPE)
        allowed = (s_part[:, None] == seg_keys[None, :])[None]
        scores = jnp.where(allowed, scores, NEG)
        row_max = jnp.max(scores, axis=-1, keepdims=True)
        expo_vals = jnp.exp(scores - row_max)
        totals = jnp.sum(expo_vals, axis=-1, keepdims=True)
        soft_weights = (expo_vals / totals).astype(HALF_TYPE)
        mixed_part = jnp.einsum(
            "hqk,khd->qhd", soft_weights, value_heads, preferred_element_type=FLOAT_TYPE
        )
        return (mixed_part.reshape(block_rows, model_width), (row_max + jnp.log(totals))[:, :, 0])

    mixed_rows, log_totals = lax.map(one_block, (q_blocks, s_blocks))
    return (mixed_rows.reshape(length, model_width), log_totals)


def attend_backward(paired):
    query_rows, key_rows, value_rows, seg_query, seg_keys, log_totals, grad_mixed = paired
    length, model_width = query_rows.shape
    head_size = model_width // HEADS
    block_rows = min(512, length)
    q_blocks = query_rows.reshape(length // block_rows, block_rows, HEADS, head_size)
    s_blocks = seg_query.reshape(length // block_rows, block_rows)
    g_blocks = grad_mixed.reshape(length // block_rows, block_rows, HEADS, head_size)
    key_heads = key_rows.reshape(-1, HEADS, head_size)
    value_heads = value_rows.reshape(-1, HEADS, head_size)

    def one_block(carried, block_items):
        grad_keys, grad_values = carried
        q_part, s_part, lse_part, g_part = block_items
        scores = jnp.einsum("qhd,khd->hqk", q_part, key_heads, preferred_element_type=FLOAT_TYPE)
        allowed = (s_part[:, None] == seg_keys[None, :])[None]
        scores = jnp.where(allowed, scores, NEG)
        soft_weights = jnp.exp(scores - lse_part[:, :, None])
        grad_values = grad_values + jnp.einsum(
            "hqk,qhd->khd",
            soft_weights.astype(HALF_TYPE),
            g_part,
            preferred_element_type=FLOAT_TYPE,
        )
        grad_soft = jnp.einsum(
            "qhd,khd->hqk", g_part, value_heads, preferred_element_type=FLOAT_TYPE
        )
        centre = jnp.sum(soft_weights * grad_soft, axis=-1, keepdims=True)
        grad_scores = (soft_weights * (grad_soft - centre)).astype(HALF_TYPE)
        grad_query = jnp.einsum(
            "hqk,khd->qhd", grad_scores, key_heads, preferred_element_type=FLOAT_TYPE
        )
        grad_keys = grad_keys + jnp.einsum(
            "hqk,qhd->khd", grad_scores, q_part, preferred_element_type=FLOAT_TYPE
        )
        return ((grad_keys, grad_values), grad_query.reshape(block_rows, model_width))

    zero_keys = jnp.zeros(key_heads.shape, FLOAT_TYPE)
    (grad_keys, grad_values), grad_query = lax.scan(
        one_block, (zero_keys, zero_keys), (q_blocks, s_blocks, log_totals, g_blocks)
    )
    return (
        grad_query.reshape(length, model_width),
        grad_keys.reshape(-1, model_width),
        grad_values.reshape(-1, model_width),
    )


def per_device(
    tokens,
    memory,
    cotangent,
    dec_segments,
    mem_segments,
    time_steps,
    time_table,
    first_gain,
    first_bias,
    self_query,
    self_key,
    self_value,
    self_out,
    cross_query,
    cross_key,
    cross_value,
    cross_out,
    second_gain,
    second_bias,
    expand_weight,
    expand_bias,
    shrink_weight,
    shrink_bias,
):
    row_count, length, model_width = tokens.shape
    mem_length = memory.shape[1]
    token_count = row_count * length
    scaling = (model_width // HEADS) ** (-0.5)
    (
        time_rows,
        gain_one,
        bias_one,
        w_query,
        w_key,
        w_value,
        w_out,
        c_query,
        c_key,
        c_value,
        c_out,
    ) = (
        lax.all_gather(time_table, "dp", axis=0, tiled=True),
        lax.all_gather(first_gain, "dp", axis=0, tiled=True),
        lax.all_gather(first_bias, "dp", axis=0, tiled=True),
        lax.all_gather(self_query, "dp", axis=0, tiled=True),
        lax.all_gather(self_key, "dp", axis=0, tiled=True),
        lax.all_gather(self_value, "dp", axis=0, tiled=True),
        lax.all_gather(self_out, "dp", axis=0, tiled=True),
        lax.all_gather(cross_query, "dp", axis=0, tiled=True),
        lax.all_gather(cross_key, "dp", axis=0, tiled=True),
        lax.all_gather(cross_value, "dp", axis=0, tiled=True),
        lax.all_gather(cross_out, "dp", axis=0, tiled=True),
    )
    slot_steps = slot_onehot(dec_segments, time_steps, time_rows.shape[1])
    input_rows = tokens.reshape(token_count, model_width).astype(FLOAT_TYPE)
    start_rows = input_rows + jnp.einsum(
        "nt,dt->nd", slot_steps, time_rows.astype(FLOAT_TYPE), precision=HIGH
    )
    normed_one, pull_one = jax.vjp(
        layer_norm, start_rows, gain_one.astype(FLOAT_TYPE), bias_one.astype(FLOAT_TYPE)
    )
    low_one = normed_one.astype(HALF_TYPE)
    query_rows = (product(low_one, w_query) * scaling).astype(HALF_TYPE)
    key_rows = product(low_one, w_key).astype(HALF_TYPE)
    value_rows = product(low_one, w_value).astype(HALF_TYPE)
    query_three = query_rows.reshape(row_count, length, model_width)
    key_three = key_rows.reshape(row_count, length, model_width)
    value_three = value_rows.reshape(row_count, length, model_width)
    self_mixed, self_lse = lax.map(
        attend_forward, (query_three, key_three, value_three, dec_segments, dec_segments)
    )
    mixed_low = self_mixed.reshape(token_count, model_width).astype(HALF_TYPE)
    after_self = start_rows + product(mixed_low, w_out)
    after_low = after_self.astype(HALF_TYPE)
    cross_q = (product(after_low, c_query) * scaling).astype(HALF_TYPE)
    memory_rows = memory.reshape(row_count * mem_length, model_width)
    cross_k = product(memory_rows, c_key).astype(HALF_TYPE)
    cross_v = product(memory_rows, c_value).astype(HALF_TYPE)
    cross_q_three = cross_q.reshape(row_count, length, model_width)
    cross_k_three = cross_k.reshape(row_count, mem_length, model_width)
    cross_v_three = cross_v.reshape(row_count, mem_length, model_width)
    cross_mixed, cross_lse = lax.map(
        attend_forward, (cross_q_three, cross_k_three, cross_v_three, dec_segments, mem_segments)
    )
    cross_low = cross_mixed.reshape(token_count, model_width).astype(HALF_TYPE)
    after_cross = after_self + product(cross_low, c_out)
    gain_two, bias_two, w_expand, b_expand, w_shrink, b_shrink = (
        lax.all_gather(second_gain, "dp", axis=0, tiled=True),
        lax.all_gather(second_bias, "dp", axis=0, tiled=True),
        lax.all_gather(expand_weight, "dp", axis=0, tiled=True),
        lax.all_gather(expand_bias, "dp", axis=0, tiled=True),
        lax.all_gather(shrink_weight, "dp", axis=0, tiled=True),
        lax.all_gather(shrink_bias, "dp", axis=0, tiled=True),
    )
    normed_two = layer_norm(after_cross, gain_two.astype(FLOAT_TYPE), bias_two.astype(FLOAT_TYPE))
    pre_act = product(normed_two.astype(HALF_TYPE), w_expand) + b_expand.astype(FLOAT_TYPE)
    act_low = exact_gelu(pre_act).astype(HALF_TYPE)
    branch = product(act_low, w_shrink) + b_shrink.astype(FLOAT_TYPE)
    keep_rows = (dec_segments.reshape(token_count, 1) >= 0).astype(FLOAT_TYPE)
    layer_out = (
        (keep_rows * (after_cross + branch))
        .astype(HALF_TYPE)
        .reshape(row_count, length, model_width)
    )
    gain_two, bias_two, w_expand, b_expand, w_shrink, b_shrink = (
        lax.all_gather(second_gain, "dp", axis=0, tiled=True),
        lax.all_gather(second_bias, "dp", axis=0, tiled=True),
        lax.all_gather(expand_weight, "dp", axis=0, tiled=True),
        lax.all_gather(expand_bias, "dp", axis=0, tiled=True),
        lax.all_gather(shrink_weight, "dp", axis=0, tiled=True),
        lax.all_gather(shrink_bias, "dp", axis=0, tiled=True),
    )
    grad_out = cotangent.reshape(token_count, model_width).astype(FLOAT_TYPE) * keep_rows
    grad_branch = grad_out.astype(HALF_TYPE)
    grad_shrink_bias = jnp.sum(grad_branch.astype(FLOAT_TYPE), axis=0)
    normed_again, pull_two = jax.vjp(
        layer_norm, after_cross, gain_two.astype(FLOAT_TYPE), bias_two.astype(FLOAT_TYPE)
    )
    low_two = normed_again.astype(HALF_TYPE)
    pre_again = product(low_two, w_expand) + b_expand.astype(FLOAT_TYPE)
    act_again, pull_act = jax.vjp(exact_gelu, pre_again)
    grad_shrink = product_left_t(act_again.astype(HALF_TYPE), grad_branch)
    grad_act = product_right_t(grad_branch, w_shrink)
    grad_pre = pull_act(grad_act)[0].astype(HALF_TYPE)
    grad_expand_bias = jnp.sum(grad_pre.astype(FLOAT_TYPE), axis=0)
    grad_expand = product_left_t(low_two, grad_pre)
    grad_low_two = product_right_t(grad_pre, w_expand)
    grad_cross_in, grad_gain_two, grad_bias_two = pull_two(grad_low_two)
    grad_after_cross = grad_out + grad_cross_in
    ffn_sums = (
        lax.psum_scatter(grad_gain_two, "dp", scatter_dimension=0, tiled=True),
        lax.psum_scatter(grad_bias_two, "dp", scatter_dimension=0, tiled=True),
        lax.psum_scatter(grad_expand, "dp", scatter_dimension=0, tiled=True),
        lax.psum_scatter(grad_expand_bias, "dp", scatter_dimension=0, tiled=True),
        lax.psum_scatter(grad_shrink, "dp", scatter_dimension=0, tiled=True),
        lax.psum_scatter(grad_shrink_bias, "dp", scatter_dimension=0, tiled=True),
    )
    w_query, w_key, w_value, w_out, c_query, c_key, c_value, c_out = (
        lax.all_gather(self_query, "dp", axis=0, tiled=True),
        lax.all_gather(self_key, "dp", axis=0, tiled=True),
        lax.all_gather(self_value, "dp", axis=0, tiled=True),
        lax.all_gather(self_out, "dp", axis=0, tiled=True),
        lax.all_gather(cross_query, "dp", axis=0, tiled=True),
        lax.all_gather(cross_key, "dp", axis=0, tiled=True),
        lax.all_gather(cross_value, "dp", axis=0, tiled=True),
        lax.all_gather(cross_out, "dp", axis=0, tiled=True),
    )
    grad_cross_branch = grad_after_cross.astype(HALF_TYPE)
    grad_c_out = product_left_t(cross_low, grad_cross_branch)
    grad_cross_mixed = product_right_t(grad_cross_branch, c_out).astype(HALF_TYPE)
    grad_cq, grad_ck, grad_cv = lax.map(
        attend_backward,
        (
            cross_q_three,
            cross_k_three,
            cross_v_three,
            dec_segments,
            mem_segments,
            cross_lse,
            grad_cross_mixed.reshape(row_count, length, model_width),
        ),
    )
    grad_cq_low = (grad_cq.reshape(token_count, model_width) * scaling).astype(HALF_TYPE)
    grad_ck_low = grad_ck.reshape(row_count * mem_length, model_width).astype(HALF_TYPE)
    grad_cv_low = grad_cv.reshape(row_count * mem_length, model_width).astype(HALF_TYPE)
    grad_c_query = product_left_t(after_low, grad_cq_low)
    grad_c_key = product_left_t(memory_rows, grad_ck_low)
    grad_c_value = product_left_t(memory_rows, grad_cv_low)
    memory_grad = (
        product_right_t(grad_ck_low, c_key) + product_right_t(grad_cv_low, c_value)
    ).reshape(row_count, mem_length, model_width)
    grad_after_self = grad_after_cross + product_right_t(grad_cq_low, c_query)
    grad_self_branch = grad_after_self.astype(HALF_TYPE)
    grad_w_out = product_left_t(mixed_low, grad_self_branch)
    grad_self_mixed = product_right_t(grad_self_branch, w_out).astype(HALF_TYPE)
    grad_sq, grad_sk, grad_sv = lax.map(
        attend_backward,
        (
            query_three,
            key_three,
            value_three,
            dec_segments,
            dec_segments,
            self_lse,
            grad_self_mixed.reshape(row_count, length, model_width),
        ),
    )
    grad_q_low = (grad_sq.reshape(token_count, model_width) * scaling).astype(HALF_TYPE)
    grad_k_low = grad_sk.reshape(token_count, model_width).astype(HALF_TYPE)
    grad_v_low = grad_sv.reshape(token_count, model_width).astype(HALF_TYPE)
    grad_w_query = product_left_t(low_one, grad_q_low)
    grad_w_key = product_left_t(low_one, grad_k_low)
    grad_w_value = product_left_t(low_one, grad_v_low)
    grad_low_one = (
        product_right_t(grad_q_low, w_query)
        + product_right_t(grad_k_low, w_key)
        + product_right_t(grad_v_low, w_value)
    )
    grad_start_norm, grad_gain_one, grad_bias_one = pull_one(grad_low_one)
    grad_start = grad_after_self + grad_start_norm
    grad_table = jnp.einsum("nd,nt->dt", grad_start, slot_steps, precision=HIGH)
    tokens_grad = grad_start.reshape(row_count, length, model_width)
    attn_sums = (
        lax.psum_scatter(grad_table, "dp", scatter_dimension=0, tiled=True),
        lax.psum_scatter(grad_gain_one, "dp", scatter_dimension=0, tiled=True),
        lax.psum_scatter(grad_bias_one, "dp", scatter_dimension=0, tiled=True),
        lax.psum_scatter(grad_w_query, "dp", scatter_dimension=0, tiled=True),
        lax.psum_scatter(grad_w_key, "dp", scatter_dimension=0, tiled=True),
        lax.psum_scatter(grad_w_value, "dp", scatter_dimension=0, tiled=True),
        lax.psum_scatter(grad_w_out, "dp", scatter_dimension=0, tiled=True),
        lax.psum_scatter(grad_c_query, "dp", scatter_dimension=0, tiled=True),
        lax.psum_scatter(grad_c_key, "dp", scatter_dimension=0, tiled=True),
        lax.psum_scatter(grad_c_value, "dp", scatter_dimension=0, tiled=True),
        lax.psum_scatter(grad_c_out, "dp", scatter_dimension=0, tiled=True),
    )
    return (
        layer_out,
        tokens_grad,
        memory_grad,
        attn_sums[0],
        attn_sums[1],
        attn_sums[2],
        attn_sums[3],
        attn_sums[4],
        attn_sums[5],
        attn_sums[6],
        attn_sums[7],
        attn_sums[8],
        attn_sums[9],
        attn_sums[10],
        ffn_sums[0],
        ffn_sums[1],
        ffn_sums[2],
        ffn_sums[3],
        ffn_sums[4],
        ffn_sums[5],
    )


def solution(mesh):
    return jax.shard_map(
        per_device,
        mesh=mesh,
        in_specs=(
            P("dp", None, None),
            P("dp", None, None),
            P("dp", None, None),
            P("dp", None),
            P("dp", None),
            P("dp", None),
            P("dp", None),
            P("dp"),
            P("dp"),
            P("dp", None),
            P("dp", None),
            P("dp", None),
            P("dp", None),
            P("dp", None),
            P("dp", None),
            P("dp", None),
            P("dp", None),
            P("dp"),
            P("dp"),
            P("dp", None),
            P("dp"),
            P("dp", None),
            P("dp"),
        ),
        out_specs=(
            P("dp", None, None),
            P("dp", None, None),
            P("dp", None, None),
            P("dp", None),
            P("dp"),
            P("dp"),
            P("dp", None),
            P("dp", None),
            P("dp", None),
            P("dp", None),
            P("dp", None),
            P("dp", None),
            P("dp", None),
            P("dp", None),
            P("dp"),
            P("dp"),
            P("dp", None),
            P("dp"),
            P("dp", None),
            P("dp"),
        ),
        check_vma=False,
    )
```

profile of v0, /device:TPU:0, one launch (start us, length us, event | category | flops | bytes accessed | tf_op | source)
XLA Modules:
  0.0 2295.6 jit_solution(11477819850531887688)
XLA Ops:
  17.2 42.1 %all-reduce.13 = (bf16[512]{0:T(512)(128)(2,1)S(1)}, bf16[512]{0:T(512)(128)(2,1)S(1)}, bf16[512]{0:T(512)(128)(2,1)S(1)}, bf16[512]{0:T(512)(128)(2,1)S(1)}, bf...) all-reduce(bf16[512]{0:T(512)(128)(2,1)S(1)} %dynamic-update-slice.1, ...), channel_id=1, replica_groups=mesh['dp'=32] {'dp'}, use_global_device_ids=true, to_apply=%add.1 | all-reduce | flops 4608 | bytes 18432
  61.2 41.5 %all_gather.64 = bf16[512,50]{1,0:T(8,128)(2,1)S(1)} all-gather(bf16[16,50]{1,0:T(8,128)(2,1)} %param.37), channel_id=1, replica_groups=mesh['dp'=32] {'dp'}, dimensions={0}, use_global_device_ids=true | all-gather | bytes 52800 | tf_op jit(solution)/shard_map/all_gather | solution.py:168
  103.7 41.2 %all_gather.67 = bf16[512,512]{1,0:T(8,128)(2,1)} all-gather(bf16[16,512]{1,0:T(8,128)(2,1)} %param.40), channel_id=1, replica_groups=mesh['dp'=32] {'dp'}, dimensions={0}, use_global_device_ids=true | all-gather | bytes 540672 | tf_op jit(solution)/shard_map/all_gather | solution.py:171
  144.9 42.0 %all_gather.68 = bf16[512,512]{1,0:T(8,128)(2,1)} all-gather(bf16[16,512]{1,0:T(8,128)(2,1)S(1)} %copy-done.84), channel_id=1, replica_groups=mesh['dp'=32] {'dp'}, dimensions={0}, use_global_device_ids=true | all-gather | bytes 540672 | tf_op jit(solution)/shard_map/all_gather | solution.py:172
  186.9 38.0 %all_gather.69 = bf16[512,512]{1,0:T(8,128)(2,1)S(1)} all-gather(bf16[16,512]{1,0:T(8,128)(2,1)S(1)} %copy-done.85), channel_id=1, replica_groups=mesh['dp'=32] {'dp'}, dimensions={0}, use_global_device_ids=true | all-gather | bytes 540672 | tf_op jit(solution)/shard_map/all_gather | solution.py:173
  225.0 42.1 %all_gather.70 = bf16[512,512]{1,0:T(8,128)(2,1)} all-gather(bf16[16,512]{1,0:T(8,128)(2,1)S(1)} %copy-done.86), channel_id=1, replica_groups=mesh['dp'=32] {'dp'}, dimensions={0}, use_global_device_ids=true | all-gather | bytes 540672 | tf_op jit(solution)/shard_map/all_gather | solution.py:174
  267.0 40.7 %all_gather.71 = bf16[512,512]{1,0:T(8,128)(2,1)} all-gather(bf16[16,512]{1,0:T(8,128)(2,1)S(1)} %copy-done.87), channel_id=1, replica_groups=mesh['dp'=32] {'dp'}, dimensions={0}, use_global_device_ids=true | all-gather | bytes 540672 | tf_op jit(solution)/shard_map/all_gather | solution.py:175
  307.7 39.6 %all_gather.72 = bf16[512,512]{1,0:T(8,128)(2,1)S(1)} all-gather(bf16[16,512]{1,0:T(8,128)(2,1)} %param.45), channel_id=1, replica_groups=mesh['dp'=32] {'dp'}, dimensions={0}, use_global_device_ids=true | all-gather | bytes 540672 | tf_op jit(solution)/shard_map/all_gather | solution.py:176
  347.4 41.0 %all_gather.73 = bf16[512,512]{1,0:T(8,128)(2,1)} all-gather(bf16[16,512]{1,0:T(8,128)(2,1)} %param.46), channel_id=1, replica_groups=mesh['dp'=32] {'dp'}, dimensions={0}, use_global_device_ids=true | all-gather | bytes 540672 | tf_op jit(solution)/shard_map/all_gather | solution.py:177
  388.3 42.2 %all_gather.74 = bf16[512,512]{1,0:T(8,128)(2,1)} all-gather(bf16[16,512]{1,0:T(8,128)(2,1)S(1)} %copy-done.88), channel_id=1, replica_groups=mesh['dp'=32] {'dp'}, dimensions={0}, use_global_device_ids=true | all-gather | bytes 540672 | tf_op jit(solution)/shard_map/all_gather | solution.py:178
  450.9 32.6 %while.94 = (s32[]{:T(128)}, bf16[2,512,512]{2,1,0:T(8,128)(2,1)}, f32[2,8,512]{2,1,0:T(8,128)S(1)}, s32[2,512]{1,0:T(2,128)S(1)}, s32[1024]{0:T(1024)S(1)}, /*i...) while((s32[]{:T(128)}, bf16[2,512,512]{2,1,0:T(8,128)(2,1)}, ...), condition=%wide.region_5.6_spmd, body=%wide.region_2.5_spmd.sunk | while | flops 1112010752 | bytes 62007440 | solution.py:74
  457.8 5.5 fusion.210
  497.6 28.3 %while.95 = (s32[]{:T(128)}, bf16[2,512,512]{2,1,0:T(8,128)(2,1)}, f32[2,8,512]{2,1,0:T(8,128)S(1)}, s32[2,512]{1,0:T(2,128)S(1)}, s32[1024]{0:T(1024)S(1)}, /*i...) while((s32[]{:T(128)}, bf16[2,512,512]{2,1,0:T(8,128)(2,1)}, ...), condition=%wide.region_9.10_spmd, body=%wide.region_6.9_spmd.sunk | while | flops 1112010752 | bytes 57813108 | solution.py:74
  529.5 24.3 %multiply_convert_fusion.2 = (bf16[1024,2048]{1,0:T(8,128)(2,1)}, f32[1024,2048]{1,0:T(8,128)}, f32[1024,2048]{1,0:T(8,128)}) fusion(f32[2048]{0:T(1024)S(1)} %copy-done.91, bf16[512,2048]{1,0:T(8,128)(2,1)} %all-gather.3.cloned.1.call-done, f32[1024,512]{0,1:T(8,128)S(1)} %get-tuple-element.702, f32[512]{0:T(512)S(1)} %copy-done.94, ...), kind=kOutput, calls=%fused_computation.90 | convolution fusion | flops 2288517120 | bytes 25186304 | tf_op jit(solution)/shard_map/dot_general | solution.py:28
  553.9 11.2 convert_reduce_fusion
  586.9 98.8 %while.96 = (s32[]{:T(128)}, f32[1024,8,64]{0,2,1:T(8,128)}, f32[1024,8,64]{0,2,1:T(8,128)}, f32[2,512,512]{2,1,0:T(8,128)}, bf16[2,512,8,64]{1,3,2,0:T(8,128)(2...) while((s32[]{:T(128)}, f32[1024,8,64]{0,2,1:T(8,128)}, ...), condition=%wide.region_16.17_spmd.clone, body=%wide.region_14.16_spmd.clone.sunk | while | flops 2737303552 | bytes 203876752 | solution.py:116
  592.4 5.7 bitcast_add_fusion.9
  598.1 11.3 multiply_reduce_fusion.10
  609.3 10.6 multiply_convert_fusion.10
  619.9 7.4 fusion.225
  640.9 6.9 bitcast_add_fusion.9
  647.8 11.3 multiply_reduce_fusion.10
  659.0 10.6 multiply_convert_fusion.10
  669.6 7.4 fusion.225
  699.9 98.7 %while.97 = (s32[]{:T(128)}, f32[1024,8,64]{0,2,1:T(8,128)}, f32[1024,8,64]{0,2,1:T(8,128)}, f32[2,512,512]{2,1,0:T(8,128)}, bf16[2,512,8,64]{1,3,2,0:T(8,128)(2...) while((s32[]{:T(128)}, f32[1024,8,64]{0,2,1:T(8,128)}, ...), condition=%wide.region_19.20_spmd.clone, body=%wide.region_17.19_spmd.clone.sunk | while | flops 2737303552 | bytes 203614544 | solution.py:116
  705.0 5.7 bitcast_add_fusion.11
  710.7 11.3 multiply_reduce_fusion.11
  722.0 10.6 multiply_convert_fusion.11
  732.6 7.4 fusion.236
  753.6 6.9 bitcast_add_fusion.11
  760.5 11.3 multiply_reduce_fusion.11
  771.7 10.6 multiply_convert_fusion.11
  782.3 7.4 fusion.236
  839.8 6.6 fusion.76
  848.0 6.6 fusion.94
  855.3 6.2 fusion.68
  864.0 37.2 %all-reduce.12 = (f32[512]{0:T(512)S(1)}, f32[512]{0:T(512)S(1)}, f32[512]{0:T(512)S(1)}, f32[512]{0:T(512)S(1)}, f32[2048]{0:T(1024)S(1)}, /*index=5*/f32[512]{0:T(512)S(1)}) all-reduce(f32[512]{0:T(512)S(1)} %get-tuple-element.590, f32[512]{0:T(512)S(1)} %get-tuple-element.592, ...), channel_id=3, replica_groups=mesh['dp'=32] {'dp'}, use_global_device_ids=true, to_apply=%region_24.25.clone | all-reduce | flops 4608 | bytes 36864
  913.9 27.5 %reduce-scatter.16.cloned.1.call-done = f32[16,50]{1,0:T(8,128)} async-done(((f32[512,50]{1,0:T(8,128)}), f32[16,50]{1,0:T(8,128)}) %reduce-scatter.16.cloned.1.call-update) | async-done | bytes 3216 | tf_op jit(solution)/shard_map/reduce_scatter | solution.py:330
  941.4 133.5 %reduce-scatter.28.cloned.1.call-done = f32[16,512]{1,0:T(8,128)} async-done(((f32[512,512]{1,0:T(8,128)}), f32[16,512]{1,0:T(8,128)}) %reduce-scatter.28.cloned.1.call-update) | async-done | bytes 32784 | tf_op jit(solution)/shard_map/reduce_scatter | solution.py:340
  1074.9 133.4 %reduce-scatter.24.cloned.1.call-done = f32[16,512]{1,0:T(8,128)} async-done(((f32[512,512]{1,0:T(8,128)}), f32[16,512]{1,0:T(8,128)}) %reduce-scatter.24.cloned.1.call-update) | async-done | bytes 32784 | tf_op jit(solution)/shard_map/reduce_scatter | solution.py:336
  1208.3 133.5 %reduce-scatter.26.cloned.1.call-done = f32[16,512]{1,0:T(8,128)} async-done(((f32[512,512]{1,0:T(8,128)}), f32[16,512]{1,0:T(8,128)}) %reduce-scatter.26.cloned.1.call-update) | async-done | bytes 32784 | tf_op jit(solution)/shard_map/reduce_scatter | solution.py:337
  1341.8 133.5 %reduce-scatter.18.cloned.1.call-done = f32[16,512]{1,0:T(8,128)} async-done(((f32[512,512]{1,0:T(8,128)}), f32[16,512]{1,0:T(8,128)}) %reduce-scatter.18.cloned.1.call-update) | async-done | bytes 32784 | tf_op jit(solution)/shard_map/reduce_scatter | solution.py:333
  1475.3 133.6 %reduce-scatter.20.cloned.1.call-done = f32[16,512]{1,0:T(8,128)} async-done(((f32[512,512]{1,0:T(8,128)}), f32[16,512]{1,0:T(8,128)}) %reduce-scatter.20.cloned.1.call-update) | async-done | bytes 32784 | tf_op jit(solution)/shard_map/reduce_scatter | solution.py:334
  1609.0 133.5 %reduce-scatter.22.cloned.1.call-done = f32[16,512]{1,0:T(8,128)} async-done(((f32[512,512]{1,0:T(8,128)}), f32[16,512]{1,0:T(8,128)}) %reduce-scatter.22.cloned.1.call-update) | async-done | bytes 32784 | tf_op jit(solution)/shard_map/reduce_scatter | solution.py:335
  1742.5 133.5 %reduce-scatter.34.cloned.1.call-done = f32[16,512]{1,0:T(8,128)} async-done(((f32[512,512]{1,0:T(8,128)}), f32[16,512]{1,0:T(8,128)}) %reduce-scatter.34.cloned.1.call-update) | async-done | bytes 32784
  1876.0 133.6 %reduce-scatter.36.cloned.1.call-done = f32[16,512]{1,0:T(8,128)} async-done(((f32[512,512]{1,0:T(8,128)}), f32[16,512]{1,0:T(8,128)}) %reduce-scatter.36.cloned.1.call-update) | async-done | bytes 32784
  2009.5 139.7 %reduce-scatter.32.cloned.1.call-done = f32[64,512]{1,0:T(8,128)} async-done(((f32[2048,512]{1,0:T(8,128)}), f32[64,512]{1,0:T(8,128)}) %reduce-scatter.32.cloned.1.call-update) | async-done | bytes 131088 | tf_op jit(solution)/shard_map/reduce_scatter | solution.py:261
  2149.2 139.6 %reduce-scatter.30.cloned.1.call-done = f32[16,2048]{1,0:T(8,128)} async-done(((f32[512,2048]{1,0:T(8,128)}), f32[16,2048]{1,0:T(8,128)}) %reduce-scatter.30.cloned.1.call-update) | async-done | bytes 131088 | tf_op jit(solution)/shard_map/reduce_scatter | solution.py:259
  (418 shorter events, 253.4 us)
Async XLA Ops:
  7.2 427.0 %copy-start = (bf16[1,1024,512]{2,1,0:T(8,128)(2,1)S(1)}, bf16[1,1024,512]{2,1,0:T(8,128)(2,1)}, u32[]{:S(2)}) copy-start(bf16[1,1024,512]{2,1,0:T(8,128)(2,1)} %param.32) | copy-start | bytes 3145732
  7.2 137.7 %copy-start.84 = (bf16[16,512]{1,0:T(8,128)(2,1)S(1)}, bf16[16,512]{1,0:T(8,128)(2,1)}, u32[]{:S(2)}) copy-start(bf16[16,512]{1,0:T(8,128)(2,1)} %param.41) | copy-start | bytes 49156
  7.2 179.7 %copy-start.85 = (bf16[16,512]{1,0:T(8,128)(2,1)S(1)}, bf16[16,512]{1,0:T(8,128)(2,1)}, u32[]{:S(2)}) copy-start(bf16[16,512]{1,0:T(8,128)(2,1)} %param.42) | copy-start | bytes 49156
  7.2 217.7 %copy-start.86 = (bf16[16,512]{1,0:T(8,128)(2,1)S(1)}, bf16[16,512]{1,0:T(8,128)(2,1)}, u32[]{:S(2)}) copy-start(bf16[16,512]{1,0:T(8,128)(2,1)} %param.43) | copy-start | bytes 49156
  7.2 259.8 %copy-start.87 = (bf16[16,512]{1,0:T(8,128)(2,1)S(1)}, bf16[16,512]{1,0:T(8,128)(2,1)}, u32[]{:S(2)}) copy-start(bf16[16,512]{1,0:T(8,128)(2,1)} %param.44) | copy-start | bytes 49156
  7.2 521.9 %all-gather.3.cloned.1.call-start = ((), (), s32[]{:S(2)}) async-start(), calls=%async_computation.11 | async-start | bytes 2162688 | tf_op jit(solution)/shard_map/all_gather | solution.py:216
  8.0 545.9 %all-gather.5.cloned.1.call-start = ((), (), s32[]{:S(2)}) async-start(), calls=%async_computation.12 | async-start | bytes 2162688 | tf_op jit(solution)/shard_map/all_gather | solution.py:218
  8.7 932.6 %reduce-scatter.16.cloned.1.call-start = ((), (), s32[]{:S(2)}) async-start(), calls=%async_computation.13 | async-start | bytes 270336 | tf_op jit(solution)/shard_map/reduce_scatter | solution.py:330
  8.9 424.4 %copy-start.29 = (bf16[2,512,512]{2,1,0:T(8,128)(2,1)}, bf16[2,512,512]{2,1,0:T(8,128)(2,1)S(1)}, u32[]{:S(2)}) copy-start(bf16[2,512,512]{2,1,0:T(8,128)(2,1)S(1)} %fusion.99) | copy-start | bytes 3145732
  59.4 329.0 %copy-start.88 = (bf16[16,512]{1,0:T(8,128)(2,1)S(1)}, bf16[16,512]{1,0:T(8,128)(2,1)}, u32[]{:S(2)}) copy-start(bf16[16,512]{1,0:T(8,128)(2,1)} %param.47) | copy-start | bytes 49156
  60.0 381.7 %copy-start.80 = (f32[512]{0:T(512)}, f32[512]{0:T(512)S(1)}, u32[]{:S(2)}) copy-start(f32[512]{0:T(512)S(1)} %convert_element_type.174) | copy-start | bytes 6148
  103.6 336.6 %copy-start.57 = (f32[1024,50]{0,1:T(8,128)}, f32[1024,50]{0,1:T(8,128)S(1)}, u32[]{:S(2)}) copy-start(f32[1024,50]{0,1:T(8,128)S(1)} %fusion.86) | copy-start | bytes 614404
  225.0 217.1 %copy-start.49 = (bf16[512,512]{1,0:T(8,128)(2,1)}, bf16[512,512]{1,0:T(8,128)(2,1)S(1)}, u32[]{:S(2)}) copy-start(bf16[512,512]{1,0:T(8,128)(2,1)S(1)} %all_gather.69) | copy-start | bytes 1572868
  347.4 89.6 %copy-start.47 = (bf16[512,512]{1,0:T(8,128)(2,1)}, bf16[512,512]{1,0:T(8,128)(2,1)S(1)}, u32[]{:S(2)}) copy-start(bf16[512,512]{1,0:T(8,128)(2,1)S(1)} %all_gather.72) | copy-start | bytes 1572868
  483.6 5.0 copy-start.37
  528.7 46.5 %copy-start.20 = (f32[1024,512]{0,1:T(8,128)}, f32[1024,512]{0,1:T(8,128)S(1)}, u32[]{:S(2)}) copy-start(f32[1024,512]{0,1:T(8,128)S(1)} %get-tuple-element.702) | copy-start | bytes 6291460
  528.8 46.5 %copy-start.71 = (f32[1024]{0:T(1024)}, f32[1024]{0:T(1024)S(1)}, u32[]{:S(2)}) copy-start(f32[1024]{0:T(1024)S(1)} %broadcast_multiply_fusion) | copy-start | bytes 12292
  529.1 46.2 %copy-start.77 = (f32[1024]{0:T(1024)}, f32[1024]{0:T(1024)S(1)}, u32[]{:S(2)}) copy-start(f32[1024]{0:T(1024)S(1)} %fusion.93) | copy-start | bytes 12292
  529.1 24.8 %copy-start.75 = (f32[1024]{0:T(1024)S(1)}, f32[1024]{0:T(1024)}, u32[]{:S(2)}) copy-start(f32[1024]{0:T(1024)} %compare_convert_fusion) | copy-start | bytes 12292
  553.9 11.2 copy-start.97
  619.9 7.4 copy-start.1
  619.9 7.4 copy-start.9
  630.2 5.6 copy-start.10
  630.2 5.6 copy-start.66
  636.5 4.4 copy-start.34
  669.6 7.4 copy-start.1
  669.6 7.4 copy-start.9
  679.9 5.6 copy-start.10
  679.9 5.6 copy-start.66
  700.6 4.4 copy-start.35
  732.6 7.4 copy-start.2
  732.6 7.4 copy-start.6
  742.9 5.6 copy-start.7
  782.3 7.4 copy-start.2
  782.3 7.4 copy-start.6
  792.6 5.6 copy-start.7
  811.6 263.3 %reduce-scatter.28.cloned.1.call-start = ((), (), s32[]{:S(2)}) async-start(), calls=%async_computation.19 | async-start | bytes 1081344 | tf_op jit(solution)/shard_map/reduce_scatter | solution.py:340
  815.0 393.3 %reduce-scatter.24.cloned.1.call-start = ((), (), s32[]{:S(2)}) async-start(), calls=%async_computation.17 | async-start | bytes 1081344 | tf_op jit(solution)/shard_map/reduce_scatter | solution.py:336
  818.0 523.8 %reduce-scatter.26.cloned.1.call-start = ((), (), s32[]{:S(2)}) async-start(), calls=%async_computation.18 | async-start | bytes 1081344 | tf_op jit(solution)/shard_map/reduce_scatter | solution.py:337
  821.7 653.6 %reduce-scatter.18.cloned.1.call-start = ((), (), s32[]{:S(2)}) async-start(), calls=%async_computation.14 | async-start | bytes 1081344 | tf_op jit(solution)/shard_map/reduce_scatter | solution.py:333
  824.8 784.1 %reduce-scatter.20.cloned.1.call-start = ((), (), s32[]{:S(2)}) async-start(), calls=%async_computation.15 | async-start | bytes 1081344 | tf_op jit(solution)/shard_map/reduce_scatter | solution.py:334
  827.9 914.6 %reduce-scatter.22.cloned.1.call-start = ((), (), s32[]{:S(2)}) async-start(), calls=%async_computation.16 | async-start | bytes 1081344 | tf_op jit(solution)/shard_map/reduce_scatter | solution.py:335
  831.4 1044.6 %reduce-scatter.34.cloned.1.call-start = ((), (), s32[]{:S(2)}) async-start(), calls=%async_computation.22 | async-start | bytes 1081344
  834.6 1174.9 %reduce-scatter.36.cloned.1.call-start = ((), (), s32[]{:S(2)}) async-start(), calls=%async_computation.23 | async-start | bytes 1081344
  839.5 1309.7 %reduce-scatter.32.cloned.1.call-start = ((), (), s32[]{:S(2)}) async-start(), calls=%async_computation.21 | async-start | bytes 4325376 | tf_op jit(solution)/shard_map/reduce_scatter | solution.py:261
  846.4 1442.5 %reduce-scatter.30.cloned.1.call-start = ((), (), s32[]{:S(2)}) async-start(), calls=%async_computation.20 | async-start | bytes 4325376 | tf_op jit(solution)/shard_map/reduce_scatter | solution.py:259
  855.3 8.7 copy-start.92
  861.5 42.6 %copy-start.17 = (f32[1024,512]{0,1:T(8,128)S(1)}, f32[1024,512]{0,1:T(8,128)}, u32[]{:S(2)}) copy-start(f32[1024,512]{0,1:T(8,128)} %copy-done.15) | copy-start | bytes 6291460
  (79 other events, 187.5 us)
Sparse Core Ops, SparseCore 0:
  10.9 59.2 all-gather.2
  73.1 56.2 all-gather.4
  811.7 129.5 reduce-scatter.15
  944.1 130.7 reduce-scatter.27
  1077.6 130.6 reduce-scatter.23
  1211.1 130.6 reduce-scatter.25
  1344.6 130.6 reduce-scatter.17
  1478.2 130.6 reduce-scatter.19
  1611.8 130.6 reduce-scatter.21
  1745.3 130.6 reduce-scatter.33
  1878.8 130.7 reduce-scatter.35
  2012.3 136.8 reduce-scatter.31
  2152.2 136.6 reduce-scatter.29
where the time goes:
time: 2300 us
  waiting for transfers between devices  1380 us (60%)
  blocking collectives  448 us (19%)
  matrix products  273 us (12%)
  local copies, waits for them, and re-layouts  98.6 us (4%)
  other arithmetic  82.1 us (4%)
    unnamed x15, waiting for transfers between devices  269 us
    reduce_scatter x1, waiting for transfers between devices, per_device(): lax.psum_scatter(grad_shrink, 'dp', scatter_dimension=0, tiled=True)  140 us
    reduce_scatter x1, waiting for transfers between devices, per_device(): lax.psum_scatter(grad_expand, 'dp', scatter_dimension=0, tiled=True)  140 us
    reduce_scatter x1, waiting for transfers between devices, per_device(): lax.psum_scatter(grad_w_key, 'dp', scatter_dimension=0, tiled=True)  134 us
    reduce_scatter x1, waiting for transfers between devices, per_device(): lax.psum_scatter(grad_c_out, 'dp', scatter_dimension=0, tiled=True)  134 us
    reduce_scatter x1, waiting for transfers between devices, per_device(): lax.psum_scatter(grad_w_value, 'dp', scatter_dimension=0, tiled=True)  134 us
    reduce_scatter x1, waiting for transfers between devices, per_device(): lax.psum_scatter(grad_w_query, 'dp', scatter_dimension=0, tiled=True)  134 us
    reduce_scatter x1, waiting for transfers between devices, per_device(): lax.psum_scatter(grad_c_query, 'dp', scatter_dimension=0, tiled=True)  133 us
  transfers between devices with their start and end apart: 13, of which 11 were waited for; matrix products, arithmetic and copies ran while one was open for 8% of the time, Pallas kernels for 0%

commit v1 on v0

v1 whole, which is shorter than its diff:
```python
import functools

import jax
import jax.numpy as jnp
from jax import lax
from jax.experimental import pallas as pl
from jax.experimental.pallas import tpu as pltpu
from jax.sharding import PartitionSpec as P

HEADS = 8
EPS = 1e-05
NEG = -1e30
F32 = jnp.float32
BF16 = jnp.bfloat16
MESH = pl.DeviceIdType.MESH
TILE = 128
VMEM_BYTES = 60 * 1024 * 1024
ROW_TILE = 256


def vmem_spec():
    return pl.BlockSpec(memory_space=pltpu.VMEM)


def smem_spec():
    return pl.BlockSpec(memory_space=pltpu.SMEM)


def hbm_spec():
    return pl.BlockSpec(memory_space=pl.ANY)


def dot(a, b):
    return lax.dot_general(a, b, (((1,), (0,)), ((), ())), preferred_element_type=F32)


def dot_nt(a, b):
    return lax.dot_general(a, b, (((1,), (1,)), ((), ())), preferred_element_type=F32)


def bit_index(bits, free, fixed):
    return tuple(slice(None) if b in free else fixed[b] for b in range(bits - 1, -1, -1))


def link_orders(bits):
    link = list(range(bits - 1, 0, -1))
    if len(link) != 4:
        return [(link, 1)]
    return [([4, 3, 2, 1], 5), ([4, 3, 1, 2], 5), ([1, 2, 4, 3], 3)]


def enter(bits, me):
    barrier = pltpu.get_barrier_semaphore()
    for b in range(bits):
        pl.semaphore_signal(barrier, inc=1, device_id=(me ^ (1 << b),), device_id_type=MESH)
    pl.semaphore_wait(barrier, bits)


def gather_kernel(bits, parts, *refs):
    ins, (one, two), (local_sem, send_sem, recv_sem) = refs[:11], refs[11:13], refs[13:]
    me = lax.axis_index("dp")
    mine = {b: lax.rem(me // (1 << b), 2) for b in range(bits)}
    own = bit_index(bits, (), mine)
    local = []
    for j in range(8):
        local.append((ins[j], one.at[(j,) + own]))
    for j in range(4):
        local.append((ins[8].at[:, pl.ds(512 * j, 512)], one.at[(8 + j,) + own]))
    local.append((ins[9], one.at[(12,) + own]))
    local.append((ins[10], two.at[own]))
    copies = [
        pltpu.make_async_copy(src, dst, local_sem.at[i]) for i, (src, dst) in enumerate(local)
    ]
    for c in copies:
        c.start()
    enter(bits, me)
    for c in copies:
        c.wait()
    bufs = (one, two)
    count = [0]
    pending = []

    def send(view, target):
        i = count[0]
        count[0] += 1
        c = pltpu.make_async_remote_copy(
            src_ref=view,
            dst_ref=view,
            send_sem=send_sem.at[i],
            recv_sem=recv_sem.at[i],
            device_id=(target,),
            device_id_type=MESH,
        )
        c.start()
        return c

    def view_of(part, free, fixed):
        which, blocks, _ = part
        index = bit_index(bits, free, fixed)
        if which == 0:
            return bufs[0].at[(slice(blocks[0], blocks[1]),) + index]
        return bufs[1].at[index + (slice(blocks[0], blocks[1]),)]

    current = []
    for part in parts:
        order = part[2]
        current.append(send(view_of(part, (), mine), me ^ (1 << order[0])))
        pending.append(send(view_of(part, (), mine), me ^ 1))
    steps = bits - 1
    for s in range(steps):
        for p, part in enumerate(parts):
            order = part[2]
            current[p].wait_recv()
            pending.append((current[p],))
            if s + 1 < steps:
                current[p] = send(
                    view_of(part, tuple(order[: s + 1]), mine), me ^ (1 << order[s + 1])
                )
            other = dict(mine)
            other[order[s]] = 1 - mine[order[s]]
            pending.append(send(view_of(part, tuple(order[:s]), other), me ^ 1))
    for c in pending:
        if isinstance(c, tuple):
            c[0].wait_send()
        else:
            c.wait()


def gather_parts(bits):
    orders = link_orders(bits)
    if len(orders) == 1:
        return [(0, (0, 13), orders[0][0]), (1, (0, 64), orders[0][0])]
    a, b, c = (o for o, _ in orders)
    return [
        (0, (0, 5), a),
        (0, (5, 10), b),
        (0, (10, 13), c),
        (1, (0, 32), a),
        (1, (32, 64), b),
    ]


def gather_all(n, arrays):
    bits = n.bit_length() - 1
    two = (2,) * bits
    parts = gather_parts(bits)
    sends = len(parts) * (2 * (bits - 1) + 1)
    return pl.pallas_call(
        functools.partial(gather_kernel, bits, parts),
        out_shape=(
            jax.ShapeDtypeStruct((13,) + two + (16, 512), BF16),
            jax.ShapeDtypeStruct(two + (64, 512), BF16),
        ),
        in_specs=[vmem_spec()] * 11,
        out_specs=(hbm_spec(), hbm_spec()),
        scratch_shapes=[
            pltpu.SemaphoreType.DMA((14,)),
            pltpu.SemaphoreType.DMA((sends,)),
            pltpu.SemaphoreType.DMA((sends,)),
        ],
        compiler_params=pltpu.CompilerParams(collective_id=0, has_side_effects=True),
        name="gather_weights",
    )(*arrays)


def scatter_kernel(bits, parts, *refs):
    attn, expand, small, two, out = refs[:5]
    r_core, work, stage_refs = refs[5], refs[6], refs[7:-2]
    send_sem, recv_sem = refs[-2:]
    me = lax.axis_index("dp")
    mine = {b: lax.rem(me // (1 << b), 2) for b in range(bits)}
    links = bits - 1
    lead = (slice(None),) * links
    enter(bits, me)
    count = [0]

    def send(src, dst, target):
        i = count[0]
        count[0] += 1
        c = pltpu.make_async_remote_copy(
            src_ref=src,
            dst_ref=dst,
            send_sem=send_sem.at[i],
            recv_sem=recv_sem.at[i],
            device_id=(target,),
            device_id_type=MESH,
        )
        c.start()
        return c

    def link_index(free, fixed):
        return tuple(slice(None) if b in free else fixed[b] for b in range(links, 0, -1))

    def send_core(part):
        blocks, _ = part
        sent = []
        low, high = blocks
        for ref, first, end in ((attn, 0, 8), (expand, 8, 12), (small, 12, 13)):
            start, stop = max(low, first), min(high, end)
            if start < stop:
                src = ref.at[(slice(start - first, stop - first),) + lead + (1 - mine[0],)]
                sent.append(send(src, r_core.at[start:stop], me ^ 1))
        for j in range(max(low, 13), high):
            src = two.at[lead + (1 - mine[0], slice(16 * (j - 13), 16 * (j - 12)))]
            sent.append(send(src, r_core.at[j], me ^ 1))
        return sent

    def positions(free):
        where = [()]
        for b in range(links, 0, -1):
            where = [w + (v,) for w in where for v in ((0, 1) if b in free else (mine[b],))]
        return where


    def add_core(part):
        low, high = part[0]
        where = positions(tuple(range(1, bits)))

        def add(j, w, own):
            work[(j,) + w] = (own.astype(F32) + r_core[(j,) + w].astype(F32)).astype(BF16)

        for ref, first, end in ((attn, 0, 8), (expand, 8, 12), (small, 12, 13)):

            def block(j, carry):
                for w in where:
                    add(j, w, ref[(j - first,) + w + (mine[0],)])
                return carry

            lax.fori_loop(max(low, first), max(low, first, min(high, end)), block, 0)
        for j in range(max(low, 13), high):
            for w in where:
                add(j, w, two[w + (mine[0], slice(16 * (j - 13), 16 * (j - 12)))])

    def send_link(part, s):
        (low, high), order = part
        free = tuple(order[s + 1 :])
        other = dict(mine)
        other[order[s]] = 1 - mine[order[s]]
        src = work.at[(slice(low, high),) + link_index(free, other)]
        return send(src, stage_refs[s].at[low:high], me ^ (1 << order[s]))

    def add_link(part, s):
        (low, high), order = part
        free = tuple(order[s + 1 :])
        where = positions(free)
        inner = [()]
        for _ in free:
            inner = [w + (v,) for w in inner for v in (0, 1)]

        def block(j, carry):
            for w, r in zip(where, inner):
                work[(j,) + w] = (
                    work[(j,) + w].astype(F32) + stage_refs[s][(j,) + r].astype(F32)
                ).astype(BF16)
            return carry

        if s + 1 < links:
            lax.fori_loop(low, high, block, 0)
            return
        for j in range(low, high):
            w = where[0]
            total = work[(j,) + w].astype(F32) + stage_refs[s][j].astype(F32)
            out[j] = total

    started = []
    current = [send_core(part) for part in parts]
    for s in range(-1, links):
        for p, part in enumerate(parts):
            for c in current[p]:
                c.wait_recv()
            started.extend(current[p])
            if s < 0:
                add_core(part)
            else:
                add_link(part, s)
            if s + 1 < links:
                current[p] = [send_link(part, s + 1)]
    for c in started:
        c.wait_send()


def scatter_sums(n, attn, expand, small, shrink):
    bits = n.bit_length() - 1
    links = bits - 1
    orders = link_orders(bits)
    if len(orders) == 1:
        parts = [((0, 17), orders[0][0][::-1])]
    else:
        a, b, c = (o[::-1] for o, _ in orders)
        parts = [((0, 7), a), ((7, 13), b), ((13, 17), c)]
    sends = len(parts) * links + 7 + len(parts)
    halves = (2,) * links
    devices = (2,) * bits
    return pl.pallas_call(
        functools.partial(scatter_kernel, bits, parts),
        out_shape=jax.ShapeDtypeStruct((17, 16, 512), F32),
        in_specs=[vmem_spec()] * 4,
        out_specs=vmem_spec(),
        scratch_shapes=[
            pltpu.VMEM((17,) + halves + (16, 512), BF16),
            pltpu.VMEM((17,) + halves + (16, 512), BF16),
        ]
        + [pltpu.VMEM((17,) + halves[: links - 1 - s] + (16, 512), BF16) for s in range(links)]
        + [pltpu.SemaphoreType.DMA((sends,)), pltpu.SemaphoreType.DMA((sends,))],
        compiler_params=pltpu.CompilerParams(
            collective_id=1, has_side_effects=True, vmem_limit_bytes=VMEM_BYTES
        ),
        name="scatter_sums",
    )(
        attn.reshape((8,) + devices + (16, 512)),
        expand.reshape((4,) + devices + (16, 512)),
        small.reshape((1,) + devices + (16, 512)),
        shrink.reshape(devices + (64, 512)),
    )


def split_kernel(sums, *outs):
    for j in range(8):
        outs[j][...] = sums[j]
    for j in range(4):
        outs[8][:, 512 * j : 512 * (j + 1)] = sums[8 + j]
        outs[9][16 * j : 16 * (j + 1), :] = sums[13 + j]
    outs[10][...] = sums[12]


def split_sums(sums):
    shapes = [(16, 512)] * 8 + [(16, 2048), (64, 512), (16, 512)]
    return pl.pallas_call(
        split_kernel,
        out_shape=tuple(jax.ShapeDtypeStruct(shape, F32) for shape in shapes),
        in_specs=[vmem_spec()],
        out_specs=tuple([vmem_spec()] * 11),
        name="split_sums",
    )(sums)


def each_tile(length, size, body):
    def step(i, carry):
        body(pl.multiple_of(i * size, size))
        return carry

    lax.fori_loop(0, length // size, step, 0)


def transpose_into(target, source, dtype=BF16):
    def tile(r):
        target[:, pl.ds(r, TILE)] = source[pl.ds(r, TILE), :].T.astype(dtype)

    each_tile(source.shape[0], TILE, tile)


def fill_columns(target, row_ref):
    def tile(r):
        row = row_ref[:, pl.ds(r, TILE)].astype(F32)
        target[pl.ds(r, TILE), :] = jnp.broadcast_to(row, (TILE, TILE)).T

    each_tile(row_ref.shape[1], TILE, tile)


def normalise(x):
    centred = x - jnp.mean(x, axis=-1, keepdims=True)
    rstd = lax.rsqrt(jnp.mean(centred * centred, axis=-1, keepdims=True) + EPS)
    return centred * rstd, rstd


def norm_backward(grad, hat, rstd, gain):
    scaled = grad * gain
    first = jnp.mean(scaled, axis=-1, keepdims=True)
    second = jnp.mean(scaled * hat, axis=-1, keepdims=True)
    return rstd * (scaled - first - hat * second)


def even_rows(shape):
    return (lax.broadcasted_iota(jnp.int32, shape, 0) & 64) == 0


def even_lanes(shape):
    return (lax.broadcasted_iota(jnp.int32, shape, 1) & 64) == 0


def mask_rows(target, block):
    even = even_rows(block.shape)
    zero = jnp.zeros_like(block)
    target[:, :TILE] = jnp.where(even, block, zero)
    target[:, TILE:] = jnp.where(even, zero, block)


def mask_lanes(target, block):
    even = even_lanes(block.shape)
    zero = jnp.zeros_like(block)
    target[:TILE, :] = jnp.where(even, block, zero)
    target[TILE:, :] = jnp.where(even, zero, block)


def attend(k_ref, q_t, v_t, key_cols, query_row, bounds, which, out_t, lse, q_pair, acc):
    width = out_t.shape[0]
    pairs = width // TILE

    def query_block(q0):
        i = q0 // TILE
        here = pl.ds(q0, TILE)
        mask_rows(q_pair, q_t[:, here])
        seg_q = query_row[:, here].astype(F32)
        acc[...] = jnp.zeros_like(acc)

        def key_block(kb, carry):
            there = pl.ds(pl.multiple_of(kb * TILE, TILE), TILE)
            bias = jnp.where(key_cols[there, :] == seg_q, 0.0, NEG)
            bias = jnp.concatenate([bias, bias], axis=1)
            result = []
            for p in range(pairs):
                lanes = slice(TILE * p, TILE * (p + 1))
                top, total = carry[p]
                scores = dot(k_ref[there, lanes], q_pair[lanes, :]) + bias
                now = jnp.maximum(top, jnp.max(scores, axis=0, keepdims=True))
                expo = jnp.exp(scores - now)
                shrink = jnp.exp(top - now)
                total = total * shrink + jnp.sum(expo, axis=0, keepdims=True)
                low = expo.astype(BF16)
                for h in range(2):
                    rows = slice(TILE * p + 64 * h, TILE * p + 64 * (h + 1))
                    cols = slice(TILE * h, TILE * (h + 1))
                    acc[rows, :] = acc[rows, :] * shrink[:, cols] + dot(
                        v_t[rows, there], low[:, cols]
                    )
                result.append((now, total))
            return tuple(result)

        start = tuple(
            (jnp.full((1, 2 * TILE), NEG, F32), jnp.zeros((1, 2 * TILE), F32))
            for _ in range(pairs)
        )
        done = lax.fori_loop(bounds[which, i], bounds[which + 1, i], key_block, start)
        for p in range(pairs):
            top, total = done[p]
            inverse = 1.0 / total
            level = top + jnp.log(total)
            for h in range(2):
                rows = slice(TILE * p + 64 * h, TILE * p + 64 * (h + 1))
                cols = slice(TILE * h, TILE * (h + 1))
                out_t[rows, here] = (acc[rows, :] * inverse[:, cols]).astype(BF16)
                lse[2 * p + h : 2 * p + h + 1, here] = level[:, cols]

    each_tile(q_t.shape[1], TILE, query_block)


def attend_back(
    q_ref, k_ref, v_ref, g_ref, q_t, k_t, g_t, out_t, lse, key_cols, query_row, bounds, which,
    scale, dq_t, dk, dv, q_rows, g_rows, q_lanes, g_lanes, acc,
):
    width = out_t.shape[0]
    pairs = width // TILE

    def clear(r):
        dk[pl.ds(r, TILE), :] = jnp.zeros((TILE, width), F32)
        dv[pl.ds(r, TILE), :] = jnp.zeros((TILE, width), F32)

    each_tile(dk.shape[0], TILE, clear)

    def query_block(q0):
        i = q0 // TILE
        here = pl.ds(q0, TILE)
        mask_rows(q_rows, q_t[:, here])
        mask_rows(g_rows, g_t[:, here])
        mask_lanes(q_lanes, q_ref[here, :])
        mask_lanes(g_lanes, g_ref[here, :])
        seg_q = query_row[:, here].astype(F32)
        acc[...] = jnp.zeros_like(acc)
        centres, levels = [], []
        for p in range(pairs):
            both = []
            for h in range(2):
                rows = slice(TILE * p + 64 * h, TILE * p + 64 * (h + 1))
                both.append(
                    jnp.sum(
                        g_t[rows, here].astype(F32) * out_t[rows, here].astype(F32),
                        axis=0,
                        keepdims=True,
                    )
                )
            centres.append(jnp.concatenate(both, axis=1))
            levels.append(
                jnp.concatenate(
                    [lse[2 * p : 2 * p + 1, here], lse[2 * p + 1 : 2 * p + 2, here]], axis=1
                )
            )

        def key_block(kb, carry):
            there = pl.ds(pl.multiple_of(kb * TILE, TILE), TILE)
            bias = jnp.where(key_cols[there, :] == seg_q, 0.0, NEG)
            bias = jnp.concatenate([bias, bias], axis=1)
            for p in range(pairs):
                lanes = slice(TILE * p, TILE * (p + 1))
                scores = dot(k_ref[there, lanes], q_rows[lanes, :]) + bias
                probs = jnp.exp(scores - levels[p])
                grads = dot(v_ref[there, lanes], g_rows[lanes, :])
                low = (probs * (grads - centres[p])).astype(BF16)
                dv[there, lanes] = dv[there, lanes] + dot(probs.astype(BF16), g_lanes[:, lanes])
                dk[there, lanes] = dk[there, lanes] + dot(low, q_lanes[:, lanes])
                for h in range(2):
                    rows = slice(TILE * p + 64 * h, TILE * p + 64 * (h + 1))
                    cols = slice(TILE * h, TILE * (h + 1))
                    acc[rows, :] = acc[rows, :] + dot(k_t[rows, there], low[:, cols])
            return carry

        lax.fori_loop(bounds[which, i], bounds[which + 1, i], key_block, 0)
        dq_t[:, here] = (acc[...] * scale).astype(BF16)

    each_tile(q_t.shape[1], TILE, query_block)


def forward_kernel(
    scale, steps, bounds, tokens, memory, dec, mem, weights, small,
    start, q, k, v, after_low, cq, ck, cv, mixed_t, lse, cross_t, cross_lse, after_cross,
    small_t, table, dec_cols, mem_cols, q_t, v_t, q_pair, acc,
):
    length, width = tokens.shape
    small_t[...] = small[:, :TILE].astype(F32).T
    table[...] = jnp.zeros_like(table)
    for s in range(steps.shape[1]):
        table[s : s + 1, :] = small_t[pl.ds(steps[0, s], 1), :]
    fill_columns(dec_cols, dec)
    fill_columns(mem_cols, mem)
    gain, offset = small_t[64:65, :], small_t[65:66, :]

    def first(r):
        rows = pl.ds(r, ROW_TILE)
        ids = lax.broadcasted_iota(jnp.int32, (ROW_TILE, TILE), 1).astype(F32)
        picks = jnp.where(dec_cols[rows, :] == ids, 1.0, 0.0).astype(BF16)
        begin = tokens[rows, :].astype(F32) + dot(picks, table[...].astype(BF16))
        start[rows, :] = begin
        hat, _ = normalise(begin)
        normed = (hat * gain + offset).astype(BF16)
        query = (dot(normed, weights[0]) * scale).astype(BF16)
        q[rows, :] = query
        q_t[:, rows] = query.T
        k[rows, :] = dot(normed, weights[1]).astype(BF16)
        value = dot(normed, weights[2]).astype(BF16)
        v[rows, :] = value
        v_t[:, rows] = value.T

    each_tile(length, ROW_TILE, first)
    attend(k, q_t, v_t, dec_cols, dec, bounds, 0, mixed_t, lse, q_pair, acc)

    def second(r):
        rows = pl.ds(r, ROW_TILE)
        after = start[rows, :] + dot(mixed_t[:, rows].T, weights[3])
        after_cross[rows, :] = after
        low = after.astype(BF16)
        after_low[rows, :] = low
        query = (dot(low, weights[4]) * scale).astype(BF16)
        cq[rows, :] = query
        q_t[:, rows] = query.T

    each_tile(length, ROW_TILE, second)

    def third(r):
        rows = pl.ds(r, ROW_TILE)
        ck[rows, :] = dot(memory[rows, :], weights[5]).astype(BF16)
        value = dot(memory[rows, :], weights[6]).astype(BF16)
        cv[rows, :] = value
        v_t[:, rows] = value.T

    each_tile(memory.shape[0], ROW_TILE, third)
    attend(ck, q_t, v_t, mem_cols, dec, bounds, 2, cross_t, cross_lse, q_pair, acc)

    def fourth(r):
        rows = pl.ds(r, ROW_TILE)
        after_cross[rows, :] = after_cross[rows, :] + dot(cross_t[:, rows].T, weights[7])

    each_tile(length, ROW_TILE, fourth)


def gelu_pair(x):
    half = 0.5 * (1.0 + lax.erf(x * 0.7071067811865476))
    density = jnp.exp(x * x * -0.5) * 0.3989422804014327
    return x * half, half + x * density


def hidden_kernel(
    after_cross, cotangent, dec, expand, shrink, small, hidden_offset,
    layer_out, grad_after, d_expand, d_shrink, d_rows, d_hidden,
    small_t, low_two, low_two_t, grad_low, act, grad_pre, dec_cols,
):
    length, width = after_cross.shape
    hidden = shrink.shape[0]
    chunk = 256
    small_t[...] = small[:, :TILE].astype(F32).T
    gain, offset, last = small_t[66:67, :], small_t[67:68, :], small_t[68:69, :]
    fill_columns(dec_cols, dec)

    def keep_rows(rows):
        keep = jnp.where(dec_cols[rows, :] >= 0.0, 1.0, 0.0)
        return jnp.concatenate([keep] * (width // TILE), axis=1)

    def first(r):
        rows = pl.ds(r, ROW_TILE)
        hat, _ = normalise(after_cross[rows, :])
        low = (hat * gain + offset).astype(BF16)
        low_two[rows, :] = low
        low_two_t[:, rows] = low.T
        grad_low[rows, :] = (cotangent[rows, :].astype(F32) * keep_rows(rows)).astype(BF16)

    each_tile(length, ROW_TILE, first)

    for c in range(hidden // chunk):
        block, inside = c * chunk // width, c * chunk % width
        lanes = slice(c * chunk, (c + 1) * chunk)

        def second(i, total):
            rows = pl.ds(pl.multiple_of(i * ROW_TILE, ROW_TILE), ROW_TILE)
            pre = dot(low_two[rows, :], expand[block, :, inside : inside + chunk])
            value, slope = gelu_pair(pre + hidden_offset[:, lanes])
            act[rows, lanes] = value.astype(BF16)
            grad = (dot_nt(grad_low[rows, :], shrink[lanes, :]) * slope).astype(BF16)
            grad_pre[rows, lanes] = grad
            return total + jnp.sum(grad.astype(F32), axis=0, keepdims=True)

        d_hidden[:, lanes] = lax.fori_loop(
            0, length // ROW_TILE, second, jnp.zeros((1, chunk), F32)
        )

    d_rows[...] = jnp.zeros_like(d_rows)

    def third(r):
        rows = pl.ds(r, ROW_TILE)
        after = after_cross[rows, :]
        branch = dot(act[rows, :], shrink[...]) + last
        keep = keep_rows(rows)
        layer_out[rows, :] = (keep * (after + branch)).astype(BF16)
        low = dot_nt(grad_pre[rows, :width], expand[0])
        for j in range(1, hidden // width):
            low = low + dot_nt(grad_pre[rows, width * j : width * (j + 1)], expand[j])
        hat, rstd = normalise(after)
        out = cotangent[rows, :].astype(F32) * keep
        grad_after[rows, :] = out + norm_backward(low, hat, rstd, gain)
        d_rows[0:1, :] = d_rows[0:1, :] + jnp.sum(low * hat, axis=0, keepdims=True)
        d_rows[1:2, :] = d_rows[1:2, :] + jnp.sum(low, axis=0, keepdims=True)
        d_rows[2:3, :] = d_rows[2:3, :] + jnp.sum(out, axis=0, keepdims=True)

    each_tile(length, ROW_TILE, third)

    for j in range(hidden // width):

        def fourth(r):
            d_expand[j, pl.ds(r, TILE), :] = dot(
                low_two_t[pl.ds(r, TILE), :], grad_pre[:, width * j : width * (j + 1)]
            ).astype(BF16)

        each_tile(width, TILE, fourth)
    for c in range(hidden // chunk):
        rows = slice(c * chunk, (c + 1) * chunk)
        d_shrink[rows, :] = dot(act[:, rows].T, grad_low[...]).astype(BF16)


def backward_kernel(
    scale, shard, steps, bounds, grad_after, memory, dec, mem, weights, small,
    start, q, k, v, after_low, cq, ck, cv, mixed_t, lse, cross_t, cross_lse, d_rows, d_hidden,
    tokens_grad, memory_grad, d_attn, d_small,
    small_t, table, dec_cols, mem_cols, g, g_t, q_t, k_t, x_t, dq_t, dk, dv, d_low, e_low,
    q_rows, g_rows, q_lanes, g_lanes, acc, small_grad,
):
    length, width = start.shape
    small_t[...] = small[:, :TILE].astype(F32).T
    fill_columns(dec_cols, dec)
    fill_columns(mem_cols, mem)
    gain, offset = small_t[64:65, :], small_t[65:66, :]
    scratch = (dq_t, dk, dv, q_rows, g_rows, q_lanes, g_lanes, acc)

    def weight_grad(index, left_t, right):
        def tile(r):
            rows = pl.ds(r, TILE)
            d_attn[index, rows, :] = dot(left_t[rows, :], right[...]).astype(BF16)

        each_tile(width, TILE, tile)

    def first(r):
        rows = pl.ds(r, ROW_TILE)
        low = grad_after[rows, :].astype(BF16)
        d_low[rows, :] = low
        mixed = dot_nt(low, weights[7]).astype(BF16)
        g[rows, :] = mixed
        g_t[:, rows] = mixed.T

    each_tile(length, ROW_TILE, first)
    weight_grad(7, cross_t, d_low)
    transpose_into(q_t, cq)
    transpose_into(k_t, ck)
    attend_back(
        cq, ck, cv, g, q_t, k_t, g_t, cross_t, cross_lse, mem_cols, dec, bounds, 2, scale, *scratch
    )
    transpose_into(x_t, memory)

    def second(r):
        rows = pl.ds(r, ROW_TILE)
        key = dk[rows, :].astype(BF16)
        value = dv[rows, :].astype(BF16)
        d_low[rows, :] = key
        e_low[rows, :] = value
        memory_grad[rows, :] = dot_nt(key, weights[5]) + dot_nt(value, weights[6])

    each_tile(memory.shape[0], ROW_TILE, second)
    weight_grad(5, x_t, d_low)
    weight_grad(6, x_t, e_low)
    transpose_into(x_t, after_low)

    def third(r):
        rows = pl.ds(r, ROW_TILE)
        low = dq_t[:, rows].T
        d_low[rows, :] = low
        after = grad_after[rows, :] + dot_nt(low, weights[4])
        tokens_grad[rows, :] = after
        low = after.astype(BF16)
        e_low[rows, :] = low
        mixed = dot_nt(low, weights[3]).astype(BF16)
        g[rows, :] = mixed
        g_t[:, rows] = mixed.T

    each_tile(length, ROW_TILE, third)
    weight_grad(4, x_t, d_low)
    weight_grad(3, mixed_t, e_low)

    transpose_into(q_t, q)
    transpose_into(k_t, k)
    attend_back(
        q, k, v, g, q_t, k_t, g_t, mixed_t, lse, dec_cols, dec, bounds, 0, scale, *scratch
    )
    small_grad[...] = jnp.zeros_like(small_grad)
    table[...] = jnp.zeros_like(table)
    ids = lax.broadcasted_iota(jnp.int32, (TILE, ROW_TILE), 0).astype(F32)

    def fourth(r):
        rows = pl.ds(r, ROW_TILE)
        query = dq_t[:, rows].T
        key = dk[rows, :].astype(BF16)
        value = dv[rows, :].astype(BF16)
        g[rows, :] = query
        d_low[rows, :] = key
        e_low[rows, :] = value
        low = dot_nt(query, weights[0]) + dot_nt(key, weights[1]) + dot_nt(value, weights[2])
        hat, rstd = normalise(start[rows, :])
        normed = (hat * gain + offset).astype(BF16)
        x_t[:, rows] = normed.T
        total = tokens_grad[rows, :] + norm_backward(low, hat, rstd, gain)
        tokens_grad[rows, :] = total
        small_grad[64:65, :] = small_grad[64:65, :] + jnp.sum(low * hat, axis=0, keepdims=True)
        small_grad[65:66, :] = small_grad[65:66, :] + jnp.sum(low, axis=0, keepdims=True)
        picks = jnp.where(dec[:, rows].astype(F32) == ids, 1.0, 0.0).astype(BF16)
        high = total.astype(BF16)
        rest = (total - high.astype(F32)).astype(BF16)
        table[...] = table[...] + dot(picks, high) + dot(picks, rest)

    each_tile(length, ROW_TILE, fourth)
    weight_grad(0, x_t, g)
    weight_grad(1, x_t, d_low)
    weight_grad(2, x_t, e_low)
    for s in range(steps.shape[1]):
        row = pl.ds(steps[0, s], 1)
        small_grad[row, :] = small_grad[row, :] + table[s : s + 1, :]
    small_grad[66:69, :] = d_rows[0:3, :]
    g_f32 = small_grad[...].T
    d_small[...] = jnp.zeros_like(d_small)
    d_small[:, :TILE] = g_f32
    per_shard = d_hidden.shape[1] * shard // width
    for d in range(width // shard):
        d_small[shard * d : shard * d + 1, TILE : TILE + per_shard] = d_hidden[
            :, per_shard * d : per_shard * (d + 1)
        ]


def compute_params():
    return pltpu.CompilerParams(vmem_limit_bytes=VMEM_BYTES)


def like(*items):
    return tuple(jax.ShapeDtypeStruct(shape, kind) for shape, kind in items)


def key_bounds(dec_row, mem_row):
    def ordered(row):
        return jnp.where(row < 0, jnp.iinfo(jnp.int32).max, row)

    query = ordered(dec_row[0])
    low, high = query[::TILE], query[TILE - 1 :: TILE]
    result = []
    for row in (dec_row, mem_row):
        keys = ordered(row[0])
        before = jnp.sum((keys[None, :] < low[:, None]).astype(jnp.int32), axis=1)
        upto = jnp.sum((keys[None, :] <= high[:, None]).astype(jnp.int32), axis=1)
        result += [before // TILE, (upto + TILE - 1) // TILE]
    return jnp.stack(result)


def small_shard(time_table, vectors, expand_bias):
    rows, steps = time_table.shape
    columns = jnp.stack(vectors, axis=1)
    wide = expand_bias.shape[0]
    lead = jnp.concatenate(
        [
            jnp.pad(time_table, ((0, 0), (0, 64 - steps))),
            jnp.pad(columns, ((0, 0), (0, 64 - len(vectors)))),
        ],
        axis=1,
    )
    hidden = jnp.pad(expand_bias[None, :], ((0, rows - 1), (0, 384 - wide)))
    return jnp.concatenate([lead, hidden], axis=1)


def per_device(
    n, tokens, memory, cotangent, dec, mem, time_steps, time_table, first_gain, first_bias,
    self_query, self_key, self_value, self_out, cross_query, cross_key, cross_value, cross_out,
    second_gain, second_bias, expand_weight, expand_bias, shrink_weight, shrink_bias,
):
    _, length, width = tokens.shape
    mem_length = memory.shape[1]
    shard = self_query.shape[0]
    hidden = n * expand_bias.shape[0]
    steps_count = time_table.shape[1]
    scale = (width // HEADS) ** (-0.5)
    attn = (
        self_query, self_key, self_value, self_out, cross_query, cross_key, cross_value, cross_out
    )
    little = small_shard(
        time_table, (first_gain, first_bias, second_gain, second_bias, shrink_bias), expand_bias
    )
    direct = shard == 16
    if direct:
        one, shrink = gather_all(n, attn + (expand_weight, little, shrink_weight))
        one = one.reshape(13, width, width)
        shrink = shrink.reshape(hidden, width)
        small = one[12]
        weights, expand = one, one
    else:
        one = jnp.stack(attn + (little,) + tuple(jnp.split(expand_weight, hidden // width, axis=1)))
        one = lax.all_gather(one, "dp", axis=1, tiled=True)
        shrink = lax.all_gather(shrink_weight, "dp", axis=0, tiled=True)
        weights, small, expand = one[:8], one[8], one[9:]
    hidden_offset = (
        small.reshape(n, shard, width)[:, 0, TILE : TILE + hidden // n].reshape(1, hidden)
    ).astype(F32)
    weights, expand = one[:8], (one[8:12] if direct else expand)
    bounds = key_bounds(dec, mem)
    row_spec = [vmem_spec()] * 2
    rows = (length, width)
    mem_rows = (mem_length, width)
    (
        start, q, k, v, after_low, cq, ck, cv, mixed_t, lse, cross_t, cross_lse, after_cross
    ) = pl.pallas_call(
        functools.partial(forward_kernel, scale),
        out_shape=like(
            (rows, F32), (rows, BF16), (rows, BF16), (rows, BF16), (rows, BF16), (rows, BF16),
            (mem_rows, BF16), (mem_rows, BF16), (rows[::-1], BF16), ((HEADS, length), F32),
            (rows[::-1], BF16), ((HEADS, length), F32), (rows, F32),
        ),
        in_specs=[smem_spec()] * 2 + [vmem_spec()] * 4 + row_spec[:1] + [vmem_spec()],
        out_specs=tuple([vmem_spec()] * 13),
        scratch_shapes=[
            pltpu.VMEM((TILE, width), F32),
            pltpu.VMEM((TILE, width), F32),
            pltpu.VMEM((length, TILE), F32),
            pltpu.VMEM((mem_length, TILE), F32),
            pltpu.VMEM((width, length), BF16),
            pltpu.VMEM((width, max(length, mem_length)), BF16),
            pltpu.VMEM((width, 2 * TILE), BF16),
            pltpu.VMEM((width, TILE), F32),
        ],
        compiler_params=compute_params(),
        name="layer_forward",
    )(time_steps, bounds, tokens[0], memory[0], dec, mem, weights, small)
    layer_out, grad_after, d_expand, d_shrink, d_rows, d_hidden = pl.pallas_call(
        hidden_kernel,
        out_shape=like(
            (rows, BF16), (rows, F32), ((hidden // width, width, width), BF16),
            ((hidden, width), BF16), ((8, width), F32), ((1, hidden), F32),
        ),
        in_specs=[vmem_spec()] * 5 + [vmem_spec(), vmem_spec()],
        out_specs=tuple([vmem_spec()] * 6),
        scratch_shapes=[
            pltpu.VMEM((TILE, width), F32),
            pltpu.VMEM(rows, BF16),
            pltpu.VMEM(rows[::-1], BF16),
            pltpu.VMEM(rows, BF16),
            pltpu.VMEM((length, hidden), BF16),
            pltpu.VMEM((length, hidden), BF16),
            pltpu.VMEM((length, TILE), F32),
        ],
        compiler_params=compute_params(),
        name="hidden_layer",
    )(after_cross, cotangent[0], dec, expand, shrink, small, hidden_offset)
    both = max(length, mem_length)
    tokens_grad, memory_grad, d_attn, d_small = pl.pallas_call(
        functools.partial(backward_kernel, scale, shard),
        out_shape=like(
            (rows, F32), (mem_rows, F32), ((8, width, width), BF16), ((width, width), F32)
        ),
        in_specs=[smem_spec()] * 2 + [vmem_spec()] * 5 + [vmem_spec()]
        + [vmem_spec()] * 14,
        out_specs=tuple([vmem_spec()] * 4),
        scratch_shapes=[
            pltpu.VMEM((TILE, width), F32),
            pltpu.VMEM((TILE, width), F32),
            pltpu.VMEM((length, TILE), F32),
            pltpu.VMEM((mem_length, TILE), F32),
            pltpu.VMEM(rows, BF16),
            pltpu.VMEM(rows[::-1], BF16),
            pltpu.VMEM(rows[::-1], BF16),
            pltpu.VMEM((width, both), BF16),
            pltpu.VMEM((width, both), BF16),
            pltpu.VMEM(rows[::-1], BF16),
            pltpu.VMEM((both, width), F32),
            pltpu.VMEM((both, width), F32),
            pltpu.VMEM((both, width), BF16),
            pltpu.VMEM((both, width), BF16),
            pltpu.VMEM((width, 2 * TILE), BF16),
            pltpu.VMEM((width, 2 * TILE), BF16),
            pltpu.VMEM((2 * TILE, width), BF16),
            pltpu.VMEM((2 * TILE, width), BF16),
            pltpu.VMEM((width, TILE), F32),
            pltpu.VMEM((TILE, width), F32),
        ],
        compiler_params=compute_params(),
        name="layer_backward",
    )(
        time_steps, bounds, grad_after, memory[0], dec, mem, weights, small, start, q, k, v,
        after_low, cq, ck, cv, mixed_t, lse, cross_t, cross_lse, d_rows, d_hidden,
    )
    if direct:
        sums = scatter_sums(n, d_attn, d_expand, d_small.astype(BF16), d_shrink)
        *d_weights, d_wide, d_tall, d_little = split_sums(sums)
    else:
        totals = lax.psum_scatter(
            jnp.concatenate([d_attn, d_expand, d_small[None].astype(BF16)]).astype(F32),
            "dp", scatter_dimension=1, tiled=True,
        )
        d_tall = lax.psum_scatter(d_shrink.astype(F32), "dp", scatter_dimension=0, tiled=True)
        d_weights = [totals[j] for j in range(8)]
        d_wide = jnp.concatenate([totals[8 + j] for j in range(hidden // width)], axis=1)
        d_little = totals[-1]
    columns = [d_little[:, 64 + j] for j in range(5)]
    return (
        layer_out[None],
        tokens_grad[None],
        memory_grad[None],
        d_little[:, :steps_count],
        columns[0],
        columns[1],
        *d_weights,
        columns[2],
        columns[3],
        d_wide,
        d_little[0, TILE : TILE + hidden // n],
        d_tall,
        columns[4],
    )


def solution(mesh):
    n = mesh.shape["dp"]
    three, two, one = P("dp", None, None), P("dp", None), P("dp")
    return jax.shard_map(
        functools.partial(per_device, n),
        mesh=mesh,
        in_specs=(three,) * 3 + (two,) * 4 + (one,) * 2 + (two,) * 8 + (one,) * 2
        + (two, one, two, one),
        out_specs=(three,) * 3 + (two,) + (one,) * 2 + (two,) * 8 + (one,) * 2
        + (two, one, two, one),
        check_vma=False,
    )
```

time: 2300 us -> 313 us (0.14)
  waiting for transfers between devices: 1380 us -> 0 us
  blocking collectives: 448 us -> 0 us
  Pallas kernels: 0 us -> 289 us
  matrix products: 273 us -> 0 us
  local copies, waits for them, and re-layouts: 98.6 us -> 18.2 us
  other arithmetic: 82.1 us -> 6.4 us
    reduce_scatter x9 -> x0, waiting for transfers between devices: 1110 us -> none  [the longest x1 140 us: per_device(): lax.psum_scatter(grad_shrink, 'dp', scatter_dimension=0, tiled=True)]
    all_gather x9 -> x0, blocking collectives: 368 us -> none  [the longest x1 42.2 us: per_device(): lax.all_gather(cross_out, 'dp', axis=0, tiled=True)]
    pallas_call x0 -> x6, Pallas kernels: none -> 289 us  [the longest x1 83.8 us: scatter_sums(): pl.pallas_call(functools.partial(scatter_kernel, bits, parts), out_shape=...]
    dot_general x61 -> x0, matrix products: 273 us -> none  [the longest x10 46.6 us: product(): return jnp.dot(left, right, preferred_element_type=FLOAT_TYPE)]
    unnamed x15 -> x0, waiting for transfers between devices: 269 us -> none
    unnamed x2 -> x0, blocking collectives: 79.3 us -> none
    convert_element_type x18 -> x2, other arithmetic: 53.5 us -> 2.1 us  [the longest x1 2.1 us: per_device(): sums = scatter_sums(n, d_attn, d_expand, d_small.astype(BF16), d_shrink)]
    unnamed x196 -> x2, local copies, waits for them, and re-layouts: 40.1 us -> 0.01 us
  transfers between devices with their start and end apart: 13 -> 0, of which waited for: 11 -> 0; matrix products, arithmetic and copies ran while one was open for 8% -> 0% of each run, Pallas kernels for 0% -> 0%
where the time goes in v1:
time: 313 us; the launch traced here: 314 us
  Pallas kernels  289 us (92%)
  local copies, waits for them, and re-layouts  18.2 us (6%)
  other arithmetic  6.4 us (2%)
    pallas_call x1, Pallas kernels, scatter_sums(): pl.pallas_call(functools.partial(scatter_kernel, bits, parts), out_shape=...  83.8 us
    pallas_call x1, Pallas kernels, per_device(): pl.pallas_call(functools.partial(backward_kernel, scale, shard), out_shap...  77.4 us
    pallas_call x1, Pallas kernels, gather_all(): pl.pallas_call(functools.partial(gather_kernel, bits, parts), out_shape=(...  54.2 us
    pallas_call x1, Pallas kernels, per_device(): pl.pallas_call(functools.partial(forward_kernel, scale), out_shape=like((...  38.3 us
    pallas_call x1, Pallas kernels, per_device(): pl.pallas_call(hidden_kernel, out_shape=like((rows, BF16), (rows, F32), (...  33.2 us
    slice x2, local copies, waits for them, and re-layouts, per_device(): weights, expand = (one[:8], one[8:12] if direct else expand)  8.22 us

profile of v1, /device:TPU:0, one launch (start us, length us, event | category | flops | bytes accessed | tf_op | source)
XLA Modules:
  0.0 314.1 jit_solution(1124924631676588421)
XLA Ops:
  0.7 0.7 compare_select_fusion.2
  1.3 0.1 slice.47
  1.4 0.1 slice.46
  1.5 0.8 copy.55
  2.3 0.7 copy.56
  3.0 0.7 copy.57
  3.8 0.7 copy.58
  4.5 0.7 copy.59
  5.3 0.1 stack.31
  5.4 0.7 compare_select_fusion
  6.1 0.7 compare_select_fusion.1
  6.7 0.2 convert_reduce_fusion.1
  7.0 0.6 pad_add_fusion.bounds
  7.6 1.4 fusion.5.refs_9_
  9.0 54.2 %gather_weights.1 = (bf16[13,2,2,2,2,2,16,512]{7,6,5,4,3,2,1,0:T(8,128)(2,1)}, bf16[2,2,2,2,2,64,512]{6,5,4,3,2,1,0:T(8,128)(2,1)}) custom-call(bf16[16,512]{1,0:T(8,128)(2,1)} %refs_0_.1, bf16[16,512]{1,0:T(8,128)(2,1)} %refs_1_.1, bf16[16,512]{1,0:T(8,128)(2,1)} %refs_2_.1, bf16[16,512]{1,0:T(8,128)(2,1)} %refs_3_.1, bf16[16,512]{1,0:T(8,128)(2,1)} %refs_4_.1, ...), custom_call_target="tpu_custom_call" | custom-call | tf_op jit(solution)/shard_map/gather_weights/pallas_call | solution.py:148
  63.2 1.1 slice.50
  64.3 0.0 copy-start
  64.3 0.7 reshape.288.hidden_offset
  65.1 3.2 %slice.51 = bf16[4,2,2,2,2,2,16,512]{7,6,5,4,3,2,1,0:T(8,128)(2,1)} slice(bf16[13,2,2,2,2,2,16,512]{7,6,5,4,3,2,1,0:T(8,128)(2,1)} %get-tuple-element.56), slice={[8:12], [0:2], [0:2], [0:2], [0:2], [0:2], [0:16], [0:512]} | slice | bytes 4194304 | tf_op jit(solution)/shard_map/slice | solution.py:841
  68.3 0.0 copy-done
  68.3 5.0 %slice.48 = bf16[8,2,2,2,2,2,16,512]{7,6,5,4,3,2,1,0:T(8,128)(2,1)} slice(bf16[13,2,2,2,2,2,16,512]{7,6,5,4,3,2,1,0:T(8,128)(2,1)} %get-tuple-element.56), slice={[0:8], [0:2], [0:2], [0:2], [0:2], [0:2], [0:16], [0:512]} | slice | bytes 8388608 | tf_op jit(solution)/shard_map/slice | solution.py:841
  73.3 38.3 %layer_forward.1 = (f32[1024,512]{1,0:T(8,128)}, bf16[1024,512]{1,0:T(8,128)(2,1)}, bf16[1024,512]{1,0:T(8,128)(2,1)}, bf16[1024,512]{1,0:T(8,128)(2,1)}, bf16[1...) custom-call(s32[1,16]{1,0:T(1,128)} %steps.3, ...), custom_call_target="tpu_custom_call" | custom-call | tf_op jit(solution)/shard_map/layer_forward/pallas_call | solution.py:848
  111.6 33.2 %hidden_layer.1 = (bf16[1024,512]{1,0:T(8,128)(2,1)}, f32[1024,512]{1,0:T(8,128)}, bf16[4,512,512]{2,1,0:T(8,128)(2,1)}, bf16[2048,512]{1,0:T(8,128)(2,1)}, f32[8,512]{1,0:T(8,128)}, /*index=5*/f32[1,2048]{1,0:T(1,128)}) custom-call(f32[1024,512]{1,0:T(8,128)} %get-tuple-element.57.after_cross, bf16[1024,512]{1,0:T(8,128)(2,1)} %bitcast.75, s32[1,1024]{1,0:T(1,128)} %dec.5, ...), custom_call_target="tpu_custom_call" | custom-call | tf_op jit(solution)/shard_map/hidden_layer/pallas_call | solution.py:870
  144.8 77.4 %layer_backward.1 = (f32[1024,512]{1,0:T(8,128)}, f32[1024,512]{1,0:T(8,128)}, bf16[8,512,512]{2,1,0:T(8,128)(2,1)}, f32[512,512]{1,0:T(8,128)}) custom-call(s32[1,16]{1,0:T(1,128)} %steps.3, s32[4,8]{1,0:T(4,128)} %pad_add_fusion.bounds, f32[1024,512]{1,0:T(8,128)} %get-tuple-element.60.grad_after, bf16[1024,512]{1,0:T(8,128)(2,1)} %bitcast.68, ...), custom_call_target="tpu_custom_call" | custom-call | tf_op jit(solution)/shard_map/layer_backward/pallas_call | solution.py:891
  222.2 2.1 convert_element_type.32
  224.3 83.8 %scatter_sums.1.sums = f32[17,16,512]{2,1,0:T(8,128)} custom-call(bf16[8,2,2,2,2,2,16,512]{7,6,5,4,3,2,1,0:T(8,128)(2,1)} %bitcast.69, bf16[4,2,2,2,2,2,16,512]{7,6,5,4,3,2,1,0:T(8,128)(2,1)} %bitcast.71, bf16[1,2,2,2,2,2,16,512]{7,6,5,4,3,2,1,0:T(8,128)(2,1)} %bitcast.70, bf16[2,2,2,2,2,64,512]{6,5,4,3,2,1,0:T(8,128)(2,1)} %bitcast.72), custom_call_target="tpu_custom_call" | custom-call | tf_op jit(solution)/shard_map/scatter_sums/pallas_call | solution.py:294
  308.1 1.8 split_sums.1
  310.0 1.2 slice_bitcast_fusion
  311.2 1.7 slice_reduce_fusion
  312.8 1.3 slice.54
  (4 shorter events, 0.0 us)
Async XLA Ops:
  64.3 4.0 %copy-start = (bf16[1,2,2,2,2,2,16,512]{7,6,5,4,3,2,1,0:T(8,128)(2,1)}, bf16[1,2,2,2,2,2,16,512]{7,6,5,4,3,2,1,0:T(8,128)(2,1)S(1)}, u32[]{:S(2)}) copy-start(bf16[1,2,2,2,2,2,16,512]{7,6,5,4,3,2,1,0:T(8,128)(2,1)S(1)} %slice.50) | copy-start | bytes 1572868
